TPU v7x, 512 devices: a whole 4x8x8 slice. The times are simulated.
512 devices in a mesh: tm: 64 (over z, y), tensor: 8 (over x, core).
Axes of the slice: x: 4, y: 8, z: 8, core: 2. Of those that a mesh axis runs over, the one named last changes fastest.
Arguments:
- frames: bfloat16 [32768, 1024], P('tm', 'tensor'), may hold values from -16 to 16
- conv_kernel: bfloat16 [31, 1024], P(None, 'tensor'), may hold values from -1 to 1
- conv_gain: float32 [1024], P('tensor'), may hold values from 0.1 to 1.9
- ffn_gain: float32 [1024], P('tensor'), may hold values from 0.1 to 1.9
- lengths: int32 [8], replicated, may hold values from 1 to 8192, 32768 in all
- routes: int32 [32768, 2], P('tm'), may hold values from 0 to 63, all different within a row; in each aligned block of 512 rows (0 to 511, 512 to 1023, ...) at most 24 rows name the same one
- route_weights: float32 [32768, 2], P('tm'), may hold values from 0.2 to 1
- w_gate: bfloat16 [64, 1024, 4096], P('tm', None, 'tensor'), may hold values from -0.1875 to 0.1875
- w_up: bfloat16 [64, 1024, 4096], P('tm', None, 'tensor'), may hold values from -0.1875 to 0.1875
- w_down: bfloat16 [64, 4096, 1024], P('tm', 'tensor'), may hold values from -0.09375 to 0.09375
Outputs:
- block_out: bfloat16 [32768, 1024], P('tm', 'tensor')
Inputs may be any that keep to these rules, and one draw needn't show every extreme that they name: `routes`: each row names 2 different experts. Among the 512 rows of one device, no expert is named more than 24 times, and in every draw some expert is named exactly 24 times there. The lengths sum to 32768; the largest is exactly 8192.
All inputs are finite; a program needn't handle non-finite values.
Results may differ from a plain program's by a relative error of at most 0.007.
Values may be sent and summed in bfloat16 or wider, within the bound.
A program may use at most 64 MiB of HBM per device.

v0:
```python
import jax
import jax.numpy as jnp
from jax import lax
from jax.sharding import PartitionSpec as P

eps = 1e-05


def padded(shard, sides, width):
    for axis, dim in sides:
        size, length = (lax.axis_size(axis), shard.shape[dim])
        up = [(i, (i + 1) % size) for i in range(size - 1)]
        down = [(j, i) for i, j in up]
        last = lax.slice_in_dim(shard, length - width, length, axis=dim)
        initial = lax.slice_in_dim(shard, 0, width, axis=dim)
        before = lax.ppermute(last, axis, up)
        after = lax.ppermute(initial, axis, down)
        shard = jnp.concatenate([before, shard, after], axis=dim)
    return shard


def segment_ids(position, lengths):
    starts = jnp.cumsum(lengths) - lengths
    return jnp.sum((position[:, None] >= starts[None, 1:]).astype(jnp.int32), axis=1)


def finish_norm(value, sums, gain, model_width):
    mean = sums[0] / model_width
    square = sums[1] / model_width
    scale = lax.rsqrt(square - mean * mean + eps)
    return ((value - mean[:, None]) * scale[:, None] * gain).astype(jnp.bfloat16)


def shards(
    frames, conv_kernel, conv_gain, ffn_gain, lengths, routes, route_weights, w_gate, w_up, w_down
):
    rows, width = frames.shape
    model_width = width * lax.axis_size("tensor")
    top = routes.shape[1]
    experts = lax.axis_size("tm") * w_gate.shape[0]
    capacity = 3 * rows // experts
    x = frames.astype(jnp.float32)
    conv_sums = lax.psum((jnp.sum(x, axis=1), jnp.sum(x * x, axis=1)), "tensor")
    normed = finish_norm(x, conv_sums, conv_gain, model_width)
    taps = conv_kernel.shape[0]
    half = (taps - 1) // 2
    extended = padded(normed, (("tm", 0),), half).astype(jnp.float32)
    position = lax.axis_index("tm") * rows + jnp.arange(rows + 2 * half, dtype=jnp.int32) - half
    segment = segment_ids(position, lengths)
    own = segment[half : half + rows]
    kernel = conv_kernel.astype(jnp.float32)
    conv = jnp.zeros((rows, width), jnp.float32)
    for tap in range(taps):
        same = own == segment[tap : tap + rows]
        conv = conv + jnp.where(same[:, None], extended[tap : tap + rows] * kernel[tap], 0.0)
    resid = x + jax.nn.silu(conv)
    ffn_sums = lax.psum((jnp.sum(resid, axis=1), jnp.sum(resid * resid, axis=1)), "tensor")
    expert_in = finish_norm(resid, ffn_sums, ffn_gain, model_width)
    names = routes.reshape(-1)
    onehot = (names[:, None] == jnp.arange(experts, dtype=jnp.int32)[None, :]).astype(jnp.int32)
    before = jnp.cumsum(onehot, axis=0) - onehot
    slots = names * capacity + jnp.sum(before * onehot, axis=1)
    gate_w = w_gate[0]
    up_w = w_up[0]
    down_w = w_down[0]
    whole = lax.all_gather(expert_in, "tensor", axis=1, tiled=True)
    table = jnp.zeros((experts * capacity, whole.shape[1]), jnp.bfloat16)
    block = lax.all_to_all(
        table.at[slots]
        .set(jnp.repeat(whole, top, axis=0))
        .reshape(experts, capacity, whole.shape[1]),
        "tm",
        split_axis=0,
        concat_axis=0,
        tiled=True,
    )
    sources, count, _ = block.shape
    flat = block.reshape(sources * count, -1)
    gate = jnp.dot(flat, gate_w, preferred_element_type=jnp.float32)
    up = jnp.dot(flat, up_w, preferred_element_type=jnp.float32)
    hidden = (jax.nn.silu(gate) * up).astype(jnp.bfloat16)
    partial_out = jnp.dot(hidden, down_w, preferred_element_type=jnp.float32)
    summed = lax.psum_scatter(
        partial_out.astype(jnp.bfloat16), "tensor", scatter_dimension=1, tiled=True
    )
    returned = lax.all_to_all(
        summed.reshape(sources, count, -1), "tm", split_axis=0, concat_axis=0, tiled=True
    )
    picked = (
        returned.reshape(experts * capacity, width)[slots]
        .astype(jnp.float32)
        .reshape(rows, top, width)
    )
    mixed = resid + jnp.sum(route_weights[:, :, None] * picked, axis=1)
    return mixed.astype(jnp.bfloat16)


def solution(mesh):
    in_specs = (
        P("tm", "tensor"),
        P(None, "tensor"),
        P("tensor"),
        P("tensor"),
        P(),
        P("tm", None),
        P("tm", None),
        P("tm", None, "tensor"),
        P("tm", None, "tensor"),
        P("tm", "tensor", None),
    )
    out_specs = P("tm", "tensor")
    return jax.shard_map(shards, mesh=mesh, in_specs=in_specs, out_specs=out_specs, check_vma=False)
```

profile of v0, /device:TPU:1, one launch (start us, length us, event | category | flops | bytes accessed | tf_op | source)
XLA Modules:
  0.0 279.1 jit_solution(6362248837994028519)
XLA Ops:
  6.5 1.2 convert_reduce_fusion
  7.7 18.7 %all-reduce.1 = (f32[512]{0:T(512)S(1)}, f32[512]{0:T(512)S(1)}) all-reduce(f32[512]{0:T(512)S(1)} %get-tuple-element.8, f32[512]{0:T(512)S(1)} %get-tuple-element.7), channel_id=1, replica_groups=mesh['tm'=64,'tensor'=8] {'tensor'}, use_global_device_ids=true, to_apply=%region_5.6 | all-reduce | flops 1024 | bytes 8192 | tf_op jit(solution)/shard_map/psum | solution.py:43
  26.4 1.1 fusion.11
  27.5 1.3 collective-permute-start
  28.8 1.3 collective-permute-start.1
  30.1 0.7 convert_element_type.45
  30.9 0.8 reduce-window.19
  31.7 0.7 bitcast_subtract_fusion
  32.3 0.1 slice.295
  32.4 0.1 convert_reduce_fusion.1
  32.5 0.1 slice_compare_fusion.29
  32.6 0.1 slice_compare_fusion.28
  32.7 0.1 slice_compare_fusion.27
  32.8 0.1 slice_compare_fusion.26
  32.8 0.3 collective-permute-done.1
  33.2 4.0 %fusion.78 = (f32[512]{0:T(512)S(1)}, f32[512]{0:T(512)S(1)}, f32[512,128]{1,0:T(8,128)S(1)}) fusion(f32[128]{0:T(128)S(1)} %get-tuple-element.17, f32[542,128]{1,0:T(8,128)S(1)} %maximum_convert_fusion, pred[512]{0:T(512)(128)(4,1)S(1)} %get-tuple-element.76, f32[128]{0:T(128)S(1)} %get-tuple-element.18, pred[512]{0:T(512)(128)(4,1)S(1)} %get-tuple-element.48, ...), kind=kLoop, calls=%fused_computation.196 | loop fusion | flops 6552576 | bytes 8555008 | tf_op jit(solution)/shard_map/reduce_sum | solution.py:57
  37.2 13.6 %all-reduce = (f32[512]{0:T(512)S(1)}, f32[512]{0:T(512)S(1)}) all-reduce(f32[512]{0:T(512)S(1)} %get-tuple-element.6, f32[512]{0:T(512)S(1)} %get-tuple-element.5), channel_id=1, replica_groups=mesh['tm'=64,'tensor'=8] {'tensor'}, use_global_device_ids=true, to_apply=%region_12.13 | all-reduce | flops 1024 | bytes 8192 | tf_op jit(solution)/shard_map/psum | solution.py:57
  50.8 0.9 multiply_convert_fusion
  51.6 0.0 all-gather.2.cloned.1.call-update
  51.6 0.0 reduce-scatter.4.cloned.1.call-start
  51.7 0.1 copy.26
  51.9 0.2 eq.150
  52.0 0.2 eq.146
  52.2 18.0 %reduce-window.20 = s32[64,8,128]{2,1,0:T(8,128)S(1)} reduce-window(s32[64,8,128]{2,1,0:T(8,128)S(1)} %fusion.76, s32[]{:T(128)} %constant.35.clone.1), window={size=1x1x128 pad=0_0x0_0x127_0}, to_apply=%region_6.7 | reduce-window | flops 8323072 | bytes 524292 | tf_op jit(solution)/shard_map/reduce-window.1
  70.2 0.1 slice.459
  70.4 0.1 copy.28
  70.6 0.1 copy.29
  70.7 0.1 copy.25
  70.8 0.2 mul.499
  71.0 0.1 broadcast_add_fusion
  71.1 0.1 fusion.15
  71.2 11.7 %all-gather.2.cloned.1.call-done = bf16[512,1024]{1,0:T(8,128)(2,1)} async-done(((bf16[512,128]{1,0:T(8,128)(2,1)}), bf16[512,1024]{1,0:T(8,128)(2,1)}) %all-gather.2.cloned.1.call-update) | async-done | bytes 1048592 | tf_op jit(solution)/shard_map/all_gather | solution.py:66
  82.9 2.3 broadcast_in_dim.271
  85.2 2.3 reshape.155
  87.5 8.1 %scatter_custom_fusion = bf16[1536,1024]{1,0:T(8,128)(2,1)} fusion(s32[1024]{0:T(1024)S(1)} %bitcast.115, bf16[1024,1024]{1,0:T(8,128)(2,1)} %reshape.155, bf16[]{:T(256)} %constant.40.clone.1), kind=kCustom, calls=%fused_computation.5 | custom fusion | bytes 3146240 | tf_op jit(solution)/shard_map/scatter | solution.py:70
  95.5 86.3 %all_to_all.10 = bf16[64,24,1024]{2,1,0:T(8,128)(2,1)S(1)} all-to-all(bf16[64,24,1024]{2,1,0:T(8,128)(2,1)} %bitcast.107), channel_id=1, replica_groups=mesh['tm'=64,'tensor'=8] {'tm'}, dimensions={0} | all-to-all | bytes 6291456 | tf_op jit(solution)/shard_map/all_to_all | solution.py:68
  181.8 1.7 copy-done.1
  183.5 3.5 %fusion.6 = f32[1536,512]{1,0:T(8,128)} fusion(bf16[1536,1024]{1,0:T(8,128)(2,1)S(1)} %bitcast.108, bf16[1,1024,512]{2,1,0:T(8,128)(2,1)S(1)} %copy-done.5), kind=kOutput, calls=%fused_computation.9 | convolution fusion | flops 1610612736 | bytes 7340032 | tf_op jit(solution)/shard_map/dot_general | solution.py:79
  187.1 8.3 %convolution_convert_fusion = bf16[1536,1024]{1,0:T(8,128)(2,1)} fusion(bf16[1536,1024]{1,0:T(8,128)(2,1)} %bitcast.109, f32[1536,512]{1,0:T(8,128)} %fusion.6, bf16[1,512,1024]{2,1,0:T(8,128)(2,1)S(1)} %copy-done, bf16[1,1024,512]{2,1,0:T(8,128)(2,1)S(1)} %copy-done.6), kind=kOutput, calls=%fused_computation.2 | convolution fusion | flops 3227516928 | bytes 11534336 | tf_op jit(solution)/shard_map/dot_general | solution.py:82
  195.4 4.7 %copy.30 = bf16[1536,1024]{0,1:T(8,128)(2,1)} copy(bf16[1536,1024]{1,0:T(8,128)(2,1)} %convolution_convert_fusion) | data formatting | bytes 6291456
  200.1 37.8 %reduce-scatter.4.cloned.1.call-done = bf16[128,1536]{1,0:T(8,128)(2,1)} async-done(((bf16[1024,1536]{1,0:T(8,128)(2,1)}), bf16[128,1536]{1,0:T(8,128)(2,1)}) %reduce-scatter.4.cloned.1.call-update) | async-done | bytes 393232
  237.9 1.9 copy.31
  239.8 12.1 %all-to-all-start.1 = ((bf16[64,24,128]{2,1,0:T(8,128)(2,1)}), bf16[64,24,128]{2,1,0:T(8,128)(2,1)S(1)}, u32[]{:S(2)}, u32[]{:S(2)}) async-start(bf16[64,24,128]{2,1,0:T(8,128)(2,1)} %bitcast.42), calls=%async_computation.1 | async-start | bytes 786432 | tf_op jit(solution)/shard_map/all_to_all | solution.py:86
  251.9 0.1 copy.24
  252.0 13.5 %all-to-all-done.1 = bf16[64,24,128]{2,1,0:T(8,128)(2,1)S(1)} async-done(((bf16[64,24,128]{2,1,0:T(8,128)(2,1)}), bf16[64,24,128]{2,1,0:T(8,128)(2,1)S(1)}, u32[]{:S(2)}, u32[]{:S(2)}) %all-to-all-start.1) | async-done | bytes 393248 | tf_op jit(solution)/shard_map/all_to_all | solution.py:86
  265.6 3.2 %gather_fusion = bf16[1024,128]{1,0:T(8,128)(2,1)S(1)} fusion(bf16[1536,128]{1,0:T(8,128)(2,1)S(1)} %bitcast.105, s32[1024]{0:T(1024)S(1)} %broadcast_clamp_fusion), kind=kCustom, calls=%fused_computation | custom fusion | bytes 528384 | tf_op jit(solution)/shard_map/gather | solution.py:90
  268.8 2.8 %fusion.8 = f32[512,128]{1,0:T(8,128)S(1)} fusion(bf16[512,2,128]{2,1,0:T(2,128)(2,1)S(1)} %bitcast.110, f32[512,2]{1,0:T(8,128)S(1)} %copy.24), kind=kLoop, calls=%fused_computation.12 | loop fusion | flops 327680 | bytes 528384 | tf_op jit(solution)/shard_map/reduce_sum | solution.py:94
  271.6 0.7 add_convert_fusion
  (29 shorter events, 0.2 us)
Async XLA Ops:
  6.5 180.5 %copy-start = (bf16[1,512,1024]{2,1,0:T(8,128)(2,1)S(1)}, bf16[1,512,1024]{2,1,0:T(8,128)(2,1)}, u32[]{:S(2)}) copy-start(bf16[1,512,1024]{2,1,0:T(8,128)(2,1)} %param.19) | copy-start | bytes 3145732
  6.5 76.4 %all-gather.2.cloned.1.call-start = ((), (), s32[]{:S(2)}) async-start(), calls=%async_computation.3 | async-start | bytes 1179648 | tf_op jit(solution)/shard_map/all_gather | solution.py:66
  27.5 5.3 %collective-permute-start = (bf16[15,128]{1,0:T(8,128)(2,1)S(1)}, bf16[15,128]{1,0:T(8,128)(2,1)S(1)}, u32[]{:S(2)}, u32[]{:S(2)}) collective-permute-start(bf16[15,128]{1,0:T(8,128)(2,1)S(1)} %get-tuple-element.14), channel_id=1, source_target_pairs={{0,8},{8,16},{16,24},{24,32},{32,40},{40,48},{48,56},{56,64},{64,7... | collective-permute-start | bytes 11528 | tf_op jit(solution)/shard_map/ppermute | solution.py:16
  28.8 4.4 %collective-permute-start.1 = (bf16[15,128]{1,0:T(8,128)(2,1)S(1)}, bf16[15,128]{1,0:T(8,128)(2,1)S(1)}, u32[]{:S(2)}, u32[]{:S(2)}) collective-permute-start(bf16[15,128]{1,0:T(8,128)(2,1)S(1)} %get-tuple-element.15), channel_id=1, source_target_pairs={{8,0},{16,8},{24,16},{32,24},{40,32},{48,40},{56,48},{64,56},{72,6... | collective-permute-start | bytes 11528 | tf_op jit(solution)/shard_map/ppermute | solution.py:17
  33.2 17.6 %copy-start.4 = (f32[128]{0:T(128)S(1)}, f32[128]{0:T(128)}, u32[]{:S(2)}) copy-start(f32[128]{0:T(128)} %param.13) | copy-start | bytes 1540
  33.2 18.5 %copy-start.2 = (s32[512,2]{0,1:T(2,128)S(1)}, s32[512,2]{0,1:T(2,128)}, u32[]{:S(2)}) copy-start(s32[512,2]{0,1:T(2,128)} %param.15) | copy-start | bytes 12292
  51.6 186.3 %reduce-scatter.4.cloned.1.call-start = ((), (), s32[]{:S(2)}) async-start(), calls=%async_computation.4 | async-start | bytes 3538944
  95.5 88.0 %copy-start.5 = (bf16[1,1024,512]{2,1,0:T(8,128)(2,1)S(1)}, bf16[1,1024,512]{2,1,0:T(8,128)(2,1)}, u32[]{:S(2)}) copy-start(bf16[1,1024,512]{2,1,0:T(8,128)(2,1)} %param.17) | copy-start | bytes 3145732
  181.8 1.7 copy-start.1
  183.5 3.6 %copy-start.6 = (bf16[1,1024,512]{2,1,0:T(8,128)(2,1)S(1)}, bf16[1,1024,512]{2,1,0:T(8,128)(2,1)}, u32[]{:S(2)}) copy-start(bf16[1,1024,512]{2,1,0:T(8,128)(2,1)} %param.18) | copy-start | bytes 3145732
  200.0 51.8 %copy-start.3 = (f32[512,2]{0,1:T(2,128)S(1)}, f32[512,2]{0,1:T(2,128)}, u32[]{:S(2)}) copy-start(f32[512,2]{0,1:T(2,128)} %param.16) | copy-start | bytes 12292
  239.8 25.8 %all-to-all-start.1 = ((bf16[64,24,128]{2,1,0:T(8,128)(2,1)}), bf16[64,24,128]{2,1,0:T(8,128)(2,1)S(1)}, u32[]{:S(2)}, u32[]{:S(2)}) async-start(bf16[64,24,128]{2,1,0:T(8,128)(2,1)} %bitcast.42), calls=%async_computation.1 | async-start | bytes 786432 | tf_op jit(solution)/shard_map/all_to_all | solution.py:86
Sparse Core Ops, SparseCore 0:
  51.8 31.0 all-gather.1
  200.2 37.6 reduce-scatter.3
where the time goes:
time: 283 us; the launch traced here: 279 us
  blocking collectives  119 us (42%)
  waiting for transfers between devices  63.4 us (22%)
  other arithmetic  31.5 us (11%)
  local copies, waits for them, and re-layouts  25.6 us (9%)
  starting transfers between devices  14.7 us (5%)
  between operations  13.7 us (5%)
  matrix products  11.8 us (4%)
    all_to_all x1, blocking collectives, shards(): lax.all_to_all(table.at[slots].set(jnp.repeat(whole, top, axis=0)).reshap...  86.3 us
    unnamed x3, waiting for transfers between devices  37.9 us
    another operation x4, other arithmetic  19 us
    psum x1, blocking collectives, shards(): conv_sums = lax.psum((jnp.sum(x, axis=1), jnp.sum(x * x, axis=1)), 'tensor')  18.7 us
    psum x1, blocking collectives, shards(): lax.psum((jnp.sum(resid, axis=1), jnp.sum(resid * resid, axis=1)), 'tensor')  13.6 us
    all_to_all x1, waiting for transfers between devices, shards(): lax.all_to_all(summed.reshape(sources, count, -1), 'tm', split_axis=0, co...  13.5 us
    all_to_all x1, starting transfers between devices, shards(): lax.all_to_all(summed.reshape(sources, count, -1), 'tm', split_axis=0, co...  12.1 us
    all_gather x1, waiting for transfers between devices, shards(): whole = lax.all_gather(expert_in, 'tensor', axis=1, tiled=True)  11.7 us
  transfers between devices with their start and end apart: 5, of which 4 were waited for; matrix products, arithmetic and copies ran while one was open for 8% of the time, Pallas kernels for 0%

commit v1 on v0

v1 whole, which is shorter than its diff:
```python
import functools
import types

import jax
import jax.numpy as jnp
from jax import lax
from jax.experimental import pallas as pl
from jax.experimental.pallas import tpu as pltpu
from jax.sharding import PartitionSpec as P

MESH = pl.DeviceIdType.MESH
EPS = 1e-05
CAP = 24
NX = 4
NZ = 8
NY = 8
F32 = jnp.float32
BF16 = jnp.bfloat16
I32 = jnp.int32


def div(a, b):
    return lax.div(a, jnp.int32(b))


def rem(a, b):
    return lax.rem(a, jnp.int32(b))


def remote(src, dst, ss, rs, dev):
    return pltpu.make_async_remote_copy(
        src_ref=src, dst_ref=dst, send_sem=ss, recv_sem=rs, device_id=dev, device_id_type=MESH
    )


def spread(row):
    return jnp.broadcast_to(row, (128, 128)).T


def row_sums(value_ref, dst_ref, groups):
    for g in range(groups):
        v = value_ref[128 * g : 128 * (g + 1), :].astype(F32).T
        dst_ref[g : g + 1, :] = jnp.sum(v, axis=0, keepdims=True)
        dst_ref[groups + g : groups + g + 1, :] = jnp.sum(v * v, axis=0, keepdims=True)


def names(rows, width, hid, depth, taps):
    groups = rows // 128
    chunks, per = NZ // 2, NY
    q = chunks * per
    crow = per * CAP
    hrow = crow // 2
    model = width * 2 * NX
    vm = pltpu.VMEM
    sem = pltpu.SemaphoreType.DMA
    return {
        "stat_s": vm((2, 2 * groups, 128), F32),
        "stat_r": vm((2, 2 * NX - 1, 2 * groups, 128), F32),
        "gain_s": vm((8, 128), F32),
        "gain_r": vm((8, 128), F32),
        "nbuf": vm((rows + 32, 128), F32),
        "halo_s": vm((2, 16, 128), BF16),
        "halo_r": vm((2, 16, 128), BF16),
        "behind": vm((rows, 128), I32),
        "ahead": vm((rows, 128), I32),
        "tapf": vm((32, 128), F32),
        "resid": vm((rows, 128), F32),
        "resid_p": vm((rows, 128), F32),
        "ein": vm((2, rows, 128), BF16),
        "pmat": vm((chunks, crow, rows), BF16),
        "dcol": vm((2, rows, 128), I32),
        "wcol": vm((2, rows, 128), F32),
        "wmat": vm((chunks, 2, rows, crow), BF16),
        "table": vm((q, 2 * CAP, 128), BF16),
        "gath": vm((NX, q, 2 * CAP, 128), BF16),
        "wg": vm((2, model, hid), BF16),
        "wu": vm((2, model, hid), BF16),
        "wd": vm((2, hid, model), BF16),
        "abuf": vm((crow, model), BF16),
        "hbuf": vm((crow, 2 * hid), BF16),
        "ybuf": vm((chunks, NX, crow, 256), F32),
        "rs_s": vm((chunks, 2, 3, hrow, 256), BF16),
        "rs_r": vm((chunks, 2, 3, hrow, 256), BF16),
        "back": vm((q, 2 * CAP, 128), BF16),
        "ret": vm((q, 2 * CAP, 128), BF16),
        "macc": vm((2, rows, 128), F32),
        "mix_r": vm((rows, 128), F32),
        "st_ss": sem((2, 2 * NX - 1)),
        "st_rs": sem((2, 2 * NX - 1)),
        "one_ss": sem((3,)),
        "one_rs": sem((3,)),
        "halo_ss": sem((2,)),
        "halo_rs": sem((2,)),
        "wl": sem((3,)),
        "w_ss": sem((3,)),
        "w_rs": sem((3,)),
        "a_ss": sem((q,)),
        "a_rs": sem((q,)),
        "g_ss": sem((chunks, 4)),
        "g_rs": sem((chunks, 4)),
        "r_ss": sem((chunks, 2, 3)),
        "r_rs": sem((chunks, 2, 3)),
        "b_ss": sem((q,)),
        "b_rs": sem((q,)),
    }


def kernel(keys, *refs):
    lengths_ref, frames_ref, taps_ref, cgain_ref, fgain_ref, routes_ref, rw_ref, wg_hbm, wu_hbm, wd_hbm, out_ref = refs[:11]
    s = types.SimpleNamespace(**dict(zip(keys, refs[11:])))
    rows, width = frames_ref.shape
    taps = taps_ref.shape[0]
    half = (taps - 1) // 2
    n_tm = NZ * NY
    n_t = 2 * NX
    model = width * n_t
    chunks = NZ // 2
    per = NY
    crow = per * CAP
    hrow = crow // 2
    groups = rows // 128

    tm = lax.axis_index("tm")
    ten = lax.axis_index("tensor")
    mz, my = div(tm, NY), rem(tm, NY)
    mx, mc = div(ten, 2), rem(ten, 2)
    oc = 1 - mc
    par = rem(my + mc, 2)
    xr, xl, xo = rem(mx + 1, NX), rem(mx + NX - 1, NX), rem(mx + 2, NX)
    peer_t = mx * 2 + rem(my, 2)
    partner = (tm, mx * 2 + oc)
    right, left = (tm, xr * 2 + mc), (tm, xl * 2 + mc)
    after, before = (rem(tm + 1, n_tm), ten), (rem(tm + n_tm - 1, n_tm), ten)

    def offsets(q):
        k, i = div(q, per), rem(q, per)
        return k + chunks * div(i, NY // 2), 2 * rem(i, NY // 2) + par

    def dest(q):
        dz, dy = offsets(q)
        return (rem(mz + dz, NZ) * NY + rem(my + dy, NY), peer_t)

    def source(q):
        dz, dy = offsets(q)
        return (rem(mz + NZ - dz, NZ) * NY + rem(my + NY - dy, NY), peer_t)

    def tensor_peer(d):
        return (tm, rem(ten + d, n_t))

    bar = pltpu.get_barrier_semaphore()

    def greet(dev):
        pl.semaphore_signal(bar, inc=1, device_id=dev, device_id_type=MESH)

    for d in range(1, n_t):
        greet(tensor_peer(d))
    greet(after)
    greet(before)

    @pl.loop(0, chunks * per)
    def _(q):
        @pl.when(q + par > 0)
        def _():
            greet(dest(q))

    hbm = (wg_hbm, wu_hbm, wd_hbm)
    wbuf = (s.wg, s.wu, s.wd)
    local_w = [pltpu.make_async_copy(hbm[i], wbuf[i].at[0], s.wl.at[i]) for i in range(3)]
    for copy in local_w:
        copy.start()
    row_sums(frames_ref, s.stat_s.at[0], groups)
    s.gain_s[...] = jnp.broadcast_to(fgain_ref[...], (8, 128))
    pl.semaphore_wait(bar, n_t - 1 + 2 + chunks * per - 1 + par)

    def stat_copies(phase):
        return [
            remote(s.stat_s.at[phase], s.stat_r.at[phase, d - 1], s.st_ss.at[phase, d - 1], s.st_rs.at[phase, d - 1], tensor_peer(d))
            for d in range(1, n_t)
        ]

    def norm_factors(phase):
        total = s.stat_s[phase]
        for d in range(n_t - 1):
            total = total + s.stat_r[phase, d]
        mean = total[0:groups] / model
        square = total[groups : 2 * groups] / model
        return mean, lax.rsqrt(square - mean * mean + EPS)

    first_stats = stat_copies(0)
    for copy in first_stats:
        copy.start()
    gain_copy = remote(s.gain_s, s.gain_r, s.one_ss.at[0], s.one_rs.at[0], partner)
    gain_copy.start()
    remote_w = [remote(hbm[i], wbuf[i].at[1], s.w_ss.at[i], s.w_rs.at[i], partner) for i in range(3)]
    for copy in remote_w:
        copy.start()

    s.tapf[0:taps, :] = taps_ref[...].astype(F32)
    starts = [jnp.int32(0)]
    for i in range(lengths_ref.shape[0]):
        starts.append(starts[-1] + lengths_ref[i])

    @pl.loop(0, groups)
    def _(g):
        r0 = pl.multiple_of(g * 128, 128)
        pos = tm * rows + r0 + lax.broadcasted_iota(I32, (128, 128), 0)
        begin = jnp.zeros((128, 128), I32)
        end = jnp.full((128, 128), n_tm * rows, I32)
        for i in range(1, len(starts) - 1):
            begin = jnp.where(pos >= starts[i], starts[i], begin)
        for i in range(len(starts) - 2, 0, -1):
            end = jnp.where(pos < starts[i], starts[i], end)
        s.behind[pl.ds(r0, 128), :] = pos - begin
        s.ahead[pl.ds(r0, 128), :] = end - 1 - pos

    n_exp = n_tm
    names_k = [routes_ref[0:1, :], routes_ref[1:2, :]]
    experts = lax.broadcasted_iota(I32, (n_exp, rows), 0)
    hot = [experts == name for name in names_k]
    both = jnp.where(hot[0] | hot[1], 1.0, 0.0).astype(BF16)
    upper = jnp.where(
        lax.broadcasted_iota(I32, (rows, rows), 0) < lax.broadcasted_iota(I32, (rows, rows), 1), 1.0, 0.0
    ).astype(BF16)
    earlier = jnp.dot(both, upper, preferred_element_type=F32)
    target = []
    for k in range(2):
        slot = jnp.sum(jnp.where(hot[k], earlier, 0.0), axis=0, keepdims=True).astype(I32)
        ez, ey = names_k[k] >> 3, names_k[k] & 7
        dz = (ez - mz + NZ) & (NZ - 1)
        dy = (ey - my + NY) & (NY - 1)
        q = (dz & (chunks - 1)) * per + (dz // chunks) * (NY // 2) + (dy >> 1)
        target.append(jnp.where((dy & 1) == par, q * CAP + slot, -1))
    place = lax.broadcasted_iota(I32, (crow, rows), 0)

    @pl.loop(0, chunks)
    def _(k):
        here = place + k * crow
        s.pmat[k] = jnp.where((here == target[0]) | (here == target[1]), 1.0, 0.0).astype(BF16)

    for copy in first_stats:
        copy.wait_recv()

    mean, scale = norm_factors(0)
    for g in range(groups):
        x = frames_ref[128 * g : 128 * (g + 1), :].astype(F32)
        n = ((x - spread(mean[g : g + 1])) * spread(scale[g : g + 1]) * cgain_ref[...]).astype(BF16)
        s.nbuf[16 + 128 * g : 16 + 128 * (g + 1), :] = n.astype(F32)
    s.halo_s[0] = s.nbuf[16:32, :].astype(BF16)
    s.halo_s[1] = s.nbuf[rows : rows + 16, :].astype(BF16)
    halos = [
        remote(s.halo_s.at[0], s.halo_r.at[0], s.halo_ss.at[0], s.halo_rs.at[0], before),
        remote(s.halo_s.at[1], s.halo_r.at[1], s.halo_ss.at[1], s.halo_rs.at[1], after),
    ]
    for copy in halos:
        copy.start()

    block = 64

    def conv(r0):
        acc = jnp.zeros((block, 128), F32)
        back_n = s.behind[pl.ds(r0, block), :]
        ahead_n = s.ahead[pl.ds(r0, block), :]
        for j in range(taps):
            d = j - half
            term = s.nbuf[pl.ds(r0 + 16 + d, block), :] * s.tapf[j : j + 1, :]
            if d < 0:
                term = jnp.where(back_n >= -d, term, 0.0)
            if d > 0:
                term = jnp.where(ahead_n >= d, term, 0.0)
            acc = acc + term
        x = frames_ref[pl.ds(r0, block), :].astype(F32)
        s.resid[pl.ds(r0, block), :] = x + acc / (1.0 + jnp.exp(-acc))

    for r0 in range(block, rows - block, block):
        conv(r0)
    for copy in halos:
        copy.wait_recv()
    s.nbuf[0:16, :] = s.halo_r[1].astype(F32)
    s.nbuf[rows + 16 : rows + 32, :] = s.halo_r[0].astype(F32)
    conv(0)
    conv(rows - block)

    resid_copy = remote(s.resid, s.resid_p, s.one_ss.at[1], s.one_rs.at[1], partner)
    resid_copy.start()
    row_sums(s.resid, s.stat_s.at[1], groups)
    second_stats = stat_copies(1)
    for copy in second_stats:
        copy.start()

    for k in range(2):
        for g in range(groups):
            lanes = slice(128 * g, 128 * (g + 1))
            s.dcol[k, lanes, :] = spread(target[k][:, lanes].astype(F32)).astype(I32)
            s.wcol[k, lanes, :] = spread(rw_ref[k : k + 1, lanes])

    gain_copy.wait_recv()
    resid_copy.wait_recv()
    for copy in second_stats:
        copy.wait_recv()
    mean, scale = norm_factors(1)
    for g in range(groups):
        m, r = spread(mean[g : g + 1]), spread(scale[g : g + 1])
        lanes = pl.ds(128 * g, 128)
        s.ein[mc, lanes, :] = ((s.resid[lanes, :] - m) * r * fgain_ref[...]).astype(BF16)
        s.ein[oc, lanes, :] = ((s.resid_p[lanes, :] - m) * r * s.gain_r[0:1, :]).astype(BF16)

    def send(q):
        return remote(s.table.at[q], s.gath.at[mx, q], s.a_ss.at[q], s.a_rs.at[q], dest(q))

    def keep(q):
        return pltpu.make_async_copy(s.table.at[q], s.gath.at[mx, q], s.a_rs.at[q])

    def pack(value):
        v = jnp.concatenate([value[:, 0:128].reshape(per, CAP, 128), value[:, 128:256].reshape(per, CAP, 128)], axis=1)
        return v.astype(BF16)

    def unpack(value):
        v = value.astype(F32)
        return v[:, :CAP, :].reshape(crow, 128).astype(BF16), v[:, CAP:, :].reshape(crow, 128).astype(BF16)

    def per_block(k, remotely, locally):
        @pl.loop(k * per, (k + 1) * per)
        def _(q):
            @pl.when(q + par > 0)
            def _():
                remotely(q)

            @pl.when(q + par == 0)
            def _():
                locally(q)

    @pl.loop(0, chunks)
    def _(k):
        both_cols = jnp.concatenate([s.ein[0], s.ein[1]], axis=1)
        picked = jnp.dot(s.pmat[k], both_cols, preferred_element_type=F32)
        s.table[pl.ds(k * per, per)] = pack(picked)
        per_block(k, lambda q: send(q).start(), lambda q: keep(q).start())

    @pl.loop(0, chunks)
    def _(k):
        here = k * crow + lax.broadcasted_iota(I32, (128, crow), 1)
        for g in range(groups):
            lanes = slice(128 * g, 128 * (g + 1))
            w = jnp.where(here == s.dcol[0, lanes, 0:1], s.wcol[0, lanes, 0:1], 0.0)
            w = w + jnp.where(here == s.dcol[1, lanes, 0:1], s.wcol[1, lanes, 0:1], 0.0)
            high = w.astype(BF16)
            s.wmat[k, 0, lanes, :] = high
            s.wmat[k, 1, lanes, :] = (w - high.astype(F32)).astype(BF16)

    s.macc[...] = jnp.zeros(s.macc.shape, F32)

    def gather_copies(k):
        whole, first, second = pl.ds(k * per, per), pl.ds(k * per, per // 2), pl.ds(k * per + per // 2, per // 2)

        def along(x, span, i, dev):
            return remote(s.gath.at[x, span], s.gath.at[x, span], s.g_ss.at[k, i], s.g_rs.at[k, i], dev)

        return (
            along(mx, whole, 0, right),
            along(mx, whole, 1, left),
            along(xl, first, 2, right),
            along(xr, second, 3, left),
        )

    def sum_copy(k, way, i):
        return remote(s.rs_s.at[k, way, i], s.rs_r.at[k, way, i], s.r_ss.at[k, way, i], s.r_rs.at[k, way, i], (right, left)[way])

    def send_back(q):
        return remote(s.back.at[q], s.ret.at[q], s.b_ss.at[q], s.b_rs.at[q], source(q))

    def keep_back(q):
        return pltpu.make_async_copy(s.back.at[q], s.ret.at[q], s.b_rs.at[q])

    for copy in local_w:
        copy.wait()
    for copy in remote_w:
        copy.wait_recv()

    def arrive(k):
        per_block(k, lambda q: send(q).wait_recv(), lambda q: keep(q).wait())
        to_right, to_left, _, _ = gather_copies(k)
        to_right.start()
        to_left.start()

    def forward(k):
        to_right, to_left, on_right, on_left = gather_copies(k)
        to_right.wait_recv()
        on_right.start()
        to_left.wait_recv()
        on_left.start()

    def experts_of(k):
        _, _, on_right, on_left = gather_copies(k)
        on_right.wait_recv()
        on_left.wait_recv()
        for x in range(NX):
            low, high = unpack(s.gath[x, pl.ds(k * per, per)])
            s.abuf[:, 256 * x : 256 * x + 128] = low
            s.abuf[:, 256 * x + 128 : 256 * x + 256] = high
        hid = s.wg.shape[2]
        for c in range(2):
            for n in range(0, hid, 256):
                gate = jnp.dot(s.abuf[...], s.wg[c, :, n : n + 256], preferred_element_type=F32)
                up = jnp.dot(s.abuf[...], s.wu[c, :, n : n + 256], preferred_element_type=F32)
                s.hbuf[:, hid * c + n : hid * c + n + 256] = (gate / (1.0 + jnp.exp(-gate)) * up).astype(BF16)
        for n in range(NX):
            cols = slice(256 * n, 256 * (n + 1))
            y = jnp.dot(s.hbuf[:, :hid], s.wd[0, :, cols], preferred_element_type=F32)
            s.ybuf[k, n] = y + jnp.dot(s.hbuf[:, hid:], s.wd[1, :, cols], preferred_element_type=F32)
        s.rs_s[k, 0, 0] = s.ybuf[k, xo, 0:hrow, :].astype(BF16)
        sum_copy(k, 0, 0).start()
        s.rs_s[k, 1, 0] = s.ybuf[k, xo, hrow:crow, :].astype(BF16)
        sum_copy(k, 1, 0).start()
        s.rs_s[k, 0, 1] = s.ybuf[k, xr, hrow:crow, :].astype(BF16)
        sum_copy(k, 0, 1).start()
        s.rs_s[k, 1, 1] = s.ybuf[k, xl, 0:hrow, :].astype(BF16)
        sum_copy(k, 1, 1).start()

    def pass_on(k):
        sum_copy(k, 0, 0).wait_recv()
        s.rs_s[k, 0, 2] = (s.ybuf[k, xr, 0:hrow, :] + s.rs_r[k, 0, 0].astype(F32)).astype(BF16)
        sum_copy(k, 0, 2).start()
        sum_copy(k, 1, 0).wait_recv()
        s.rs_s[k, 1, 2] = (s.ybuf[k, xl, hrow:crow, :] + s.rs_r[k, 1, 0].astype(F32)).astype(BF16)
        sum_copy(k, 1, 2).start()

    def finish(k):
        for way in range(2):
            sum_copy(k, way, 1).wait_recv()
            sum_copy(k, way, 2).wait_recv()
        top = s.ybuf[k, mx, 0:hrow, :] + s.rs_r[k, 0, 2].astype(F32) + s.rs_r[k, 1, 1].astype(F32)
        low = s.ybuf[k, mx, hrow:crow, :] + s.rs_r[k, 1, 2].astype(F32) + s.rs_r[k, 0, 1].astype(F32)
        s.back[pl.ds(k * per, per)] = pack(jnp.concatenate([top, low], axis=0))
        per_block(k, lambda q: send_back(q).start(), lambda q: keep_back(q).start())

    def combine(k):
        per_block(k, lambda q: send_back(q).wait_recv(), lambda q: keep_back(q).wait())
        low, high = unpack(s.ret[pl.ds(k * per, per)])
        both_cols = jnp.concatenate([low, high], axis=1)
        mixed = jnp.dot(s.wmat[k, 0], both_cols, preferred_element_type=F32)
        mixed = mixed + jnp.dot(s.wmat[k, 1], both_cols, preferred_element_type=F32)
        s.macc[0] += mixed[:, 0:128]
        s.macc[1] += mixed[:, 128:256]

    def at(step, lag, stage):
        @pl.when((step >= lag) & (step < lag + chunks))
        def _():
            stage(step - lag)

    @pl.loop(0, chunks + 5)
    def _(step):
        at(step, 0, arrive)
        at(step, 1, forward)
        at(step, 3, pass_on)
        at(step, 4, finish)
        at(step, 2, experts_of)
        at(step, 5, combine)

    mix_copy = remote(s.macc.at[oc], s.mix_r, s.one_ss.at[2], s.one_rs.at[2], partner)
    mix_copy.start()
    own = s.resid[...] + s.macc[mc]
    mix_copy.wait_recv()
    out_ref[...] = (own + s.mix_r[...]).astype(BF16)

    for copy in first_stats + second_stats + [gain_copy, resid_copy, mix_copy] + remote_w + halos:
        copy.wait_send()

    def left_q(q):
        send(q).wait_send()
        send_back(q).wait_send()

    @pl.loop(0, chunks)
    def _(k):
        per_block(k, left_q, lambda q: None)
        for copy in gather_copies(k):
            copy.wait_send()
        for way in range(2):
            for i in range(3):
                sum_copy(k, way, i).wait_send()


def shards(frames, conv_kernel, conv_gain, ffn_gain, lengths, routes, route_weights, w_gate, w_up, w_down):
    rows, width = frames.shape
    _, depth, hid = w_gate.shape
    scratch = names(rows, width, hid, depth, conv_kernel.shape[0])
    vmem = pl.BlockSpec(memory_space=pltpu.VMEM)
    return pl.pallas_call(
        functools.partial(kernel, tuple(scratch)),
        out_shape=jax.ShapeDtypeStruct((rows, width), BF16),
        in_specs=[pl.BlockSpec(memory_space=pltpu.SMEM)] + [vmem] * 6 + [pl.BlockSpec(memory_space=pl.ANY)] * 3,
        out_specs=vmem,
        scratch_shapes=list(scratch.values()),
        compiler_params=pltpu.CompilerParams(collective_id=0, has_side_effects=True, vmem_limit_bytes=56 * 1024 * 1024),
    )(
        lengths,
        frames,
        conv_kernel,
        conv_gain.reshape(1, width),
        ffn_gain.reshape(1, width),
        routes.T,
        route_weights.T,
        w_gate.reshape(depth, hid),
        w_up.reshape(depth, hid),
        w_down.reshape(hid, depth),
    )


def solution(mesh):
    in_specs = (
        P("tm", "tensor"),
        P(None, "tensor"),
        P("tensor"),
        P("tensor"),
        P(),
        P("tm", None),
        P("tm", None),
        P("tm", None, "tensor"),
        P("tm", None, "tensor"),
        P("tm", "tensor", None),
    )
    return jax.shard_map(shards, mesh=mesh, in_specs=in_specs, out_specs=P("tm", "tensor"), check_vma=False)
```

time: 283 us -> 85.7 us (0.30); the launches traced: 279 us -> 85.5 us
  blocking collectives: 119 us -> 0 us
  Pallas kernels: 0 us -> 83.9 us
  waiting for transfers between devices: 63.4 us -> 0 us
  other arithmetic: 31.5 us -> 0 us
  local copies, waits for them, and re-layouts: 25.6 us -> 1.57 us
  starting transfers between devices: 14.7 us -> 0 us
  between operations: 13.7 us -> 0.01 us
  matrix products: 11.8 us -> 0 us
    all_to_all x1 -> x0, blocking collectives: 86.3 us -> none  [shards(): lax.all_to_all(table.at[slots].set(jnp.repeat(whole, top, axis=0)).reshap...]
    pallas_call x0 -> x1, Pallas kernels: none -> 83.9 us  [shards(): pl.pallas_call(functools.partial(kernel, tuple(scratch)), out_shape=jax.S...]
    unnamed x3 -> x0, waiting for transfers between devices: 37.9 us -> none
    psum x2 -> x0, blocking collectives: 32.2 us -> none  [the longest x1 18.7 us: shards(): conv_sums = lax.psum((jnp.sum(x, axis=1), jnp.sum(x * x, axis=1)), 'tensor')]
    another operation x4 -> x0, other arithmetic: 19 us -> none
    all_to_all x1 -> x0, waiting for transfers between devices: 13.5 us -> none  [shards(): lax.all_to_all(summed.reshape(sources, count, -1), 'tm', split_axis=0, co...]
    all_to_all x1 -> x0, starting transfers between devices: 12.1 us -> none  [shards(): lax.all_to_all(summed.reshape(sources, count, -1), 'tm', split_axis=0, co...]
    dot_general x2 -> x0, matrix products: 11.8 us -> none  [the longest x1 8.27 us: shards(): partial_out = jnp.dot(hidden, down_w, preferred_element_type=jnp.float32)]
  transfers between devices with their start and end apart: 5 -> 0, of which waited for: 4 -> 0; matrix products, arithmetic and copies ran while one was open for 8% -> 0% of each run, Pallas kernels for 0% -> 0%
where the time goes in v1:
time: 85.7 us; the launch traced here: 85.5 us
  Pallas kernels  83.9 us (98%)
  local copies, waits for them, and re-layouts  1.57 us (2%)
    pallas_call x1, Pallas kernels, shards(): pl.pallas_call(functools.partial(kernel, tuple(scratch)), out_shape=jax.S...  83.9 us

profile of v1, /device:TPU:1, one launch (start us, length us, event | category | flops | bytes accessed | tf_op | source)
XLA Modules:
  0.0 85.5 jit_solution(8032303142162793606)
XLA Ops:
  0.0 83.9 %shard_map.100 = bf16[512,128]{1,0:T(8,128)(2,1)} custom-call(s32[8]{0:T(128)} %refs_0_.1, bf16[512,128]{1,0:T(8,128)(2,1)} %refs_1_.1, bf16[31,128]{1,0:T(8,128)(2,1)} %refs_2_.1, f32[1,128]{1,0:T(1,128)} %bitcast.12, f32[1,128]{1,0:T(1,128)} %bitcast.13, s32[2,512]{1,0:T(2,128)} %bitcast.10, f32[2,512]{1,0:T(2,128)} %bitcast.11, ...), custom_call_target="tpu_custom_call" | custom-call | tf_op jit(solution)/shard_map/pallas_call | solution.py:487
  84.0 1.6 %copy.12 = bf16[512,128]{1,0:T(8,128)(2,1)} copy(bf16[512,128]{1,0:T(8,128)(2,1)} %shard_map.100) | data formatting | bytes 262144

commit v2 on v1

--- a/solution.py
+++ b/solution.py
@@ -14,6 +14,8 @@
 NX = 4
 NZ = 8
 NY = 8
+ORDER = (4, 3, 2, 0, 1, 7, 6, 5)
+LAGS = (2, 6, 9, 12, 17)
 F32 = jnp.float32
 BF16 = jnp.bfloat16
 I32 = jnp.int32
@@ -31,6 +33,10 @@
     return pltpu.make_async_remote_copy(
         src_ref=src, dst_ref=dst, send_sem=ss, recv_sem=rs, device_id=dev, device_id_type=MESH
     )
+
+
+def wait_all(ref, sem):
+    pltpu.make_async_copy(ref, ref, sem).wait()
 
 
 def spread(row):
@@ -44,9 +50,9 @@
         dst_ref[groups + g : groups + g + 1, :] = jnp.sum(v * v, axis=0, keepdims=True)
 
 
-def names(rows, width, hid, depth, taps):
+def names(rows, width, hid, depth, taps, lens):
     groups = rows // 128
-    chunks, per = NZ // 2, NY
+    chunks, per = NZ, NY // 2
     q = chunks * per
     crow = per * CAP
     hrow = crow // 2
@@ -54,12 +60,20 @@
     vm = pltpu.VMEM
     sem = pltpu.SemaphoreType.DMA
     return {
+        "lens": pltpu.SMEM((lens,), I32),
+        "frames": vm((rows, width), BF16),
+        "taps": vm((taps, width), BF16),
+        "cgain": vm((1, width), F32),
+        "fgain": vm((1, width), F32),
+        "routes": vm((2, rows), I32),
+        "rw": vm((2, rows), F32),
+        "in_sem": sem((7,)),
         "stat_s": vm((2, 2 * groups, 128), F32),
         "stat_r": vm((2, 2 * NX - 1, 2 * groups, 128), F32),
         "gain_s": vm((8, 128), F32),
         "gain_r": vm((8, 128), F32),
         "nbuf": vm((rows + 32, 128), F32),
-        "halo_s": vm((2, 16, 128), BF16),
+        "edge_r": vm((2, 2 * NX, 2 * groups, 128), F32),
         "halo_r": vm((2, 16, 128), BF16),
         "behind": vm((rows, 128), I32),
         "ahead": vm((rows, 128), I32),
@@ -79,43 +93,53 @@
         "abuf": vm((crow, model), BF16),
         "hbuf": vm((crow, 2 * hid), BF16),
         "ybuf": vm((chunks, NX, crow, 256), F32),
-        "rs_s": vm((chunks, 2, 3, hrow, 256), BF16),
-        "rs_r": vm((chunks, 2, 3, hrow, 256), BF16),
+        "rs_s": vm((chunks, 3, 2, hrow, 256), BF16),
+        "rs_r": vm((chunks, 3, 2, hrow, 256), BF16),
         "back": vm((q, 2 * CAP, 128), BF16),
         "ret": vm((q, 2 * CAP, 128), BF16),
         "macc": vm((2, rows, 128), F32),
         "mix_r": vm((rows, 128), F32),
-        "st_ss": sem((2, 2 * NX - 1)),
-        "st_rs": sem((2, 2 * NX - 1)),
+        "st_ss": sem((2,)),
+        "st_rs": sem((2,)),
         "one_ss": sem((3,)),
         "one_rs": sem((3,)),
-        "halo_ss": sem((2,)),
-        "halo_rs": sem((2,)),
+        "edge_ss": sem((2,)),
+        "edge_rs": sem((2,)),
         "wl": sem((3,)),
         "w_ss": sem((3,)),
         "w_rs": sem((3,)),
-        "a_ss": sem((q,)),
-        "a_rs": sem((q,)),
-        "g_ss": sem((chunks, 4)),
-        "g_rs": sem((chunks, 4)),
-        "r_ss": sem((chunks, 2, 3)),
-        "r_rs": sem((chunks, 2, 3)),
-        "b_ss": sem((q,)),
-        "b_rs": sem((q,)),
+        "a_ss": sem((1,)),
+        "a_rs": sem((chunks,)),
+        "g_ss": sem((1,)),
+        "g_rs": sem((chunks, 2)),
+        "r_ss": sem((1,)),
+        "r_rs": sem((chunks, 2)),
+        "b_ss": sem((1,)),
+        "b_rs": sem((chunks,)),
     }
 
 
 def kernel(keys, *refs):
-    lengths_ref, frames_ref, taps_ref, cgain_ref, fgain_ref, routes_ref, rw_ref, wg_hbm, wu_hbm, wd_hbm, out_ref = refs[:11]
+    inputs, (wg_hbm, wu_hbm, wd_hbm, out_ref) = refs[:7], refs[7:11]
     s = types.SimpleNamespace(**dict(zip(keys, refs[11:])))
+    frames_ref, taps_ref, cgain_ref, fgain_ref = s.frames, s.taps, s.cgain, s.fgain
+    lengths_ref, routes_ref, rw_ref = s.lens, s.routes, s.rw
+    brought = [
+        pltpu.make_async_copy(src, dst, s.in_sem.at[i])
+        for i, (src, dst) in enumerate(
+            zip(inputs, (lengths_ref, frames_ref, taps_ref, cgain_ref, fgain_ref, routes_ref, rw_ref))
+        )
+    ]
+    for i in (1, 0, 2, 3, 4, 5, 6):
+        brought[i].start()
     rows, width = frames_ref.shape
     taps = taps_ref.shape[0]
     half = (taps - 1) // 2
     n_tm = NZ * NY
     n_t = 2 * NX
     model = width * n_t
-    chunks = NZ // 2
-    per = NY
+    chunks = NZ
+    per = NY // 2
     crow = per * CAP
     hrow = crow // 2
     groups = rows // 128
@@ -126,15 +150,19 @@
     mx, mc = div(ten, 2), rem(ten, 2)
     oc = 1 - mc
     par = rem(my + mc, 2)
+    own_q = ORDER.index(0) * per
     xr, xl, xo = rem(mx + 1, NX), rem(mx + NX - 1, NX), rem(mx + 2, NX)
     peer_t = mx * 2 + rem(my, 2)
     partner = (tm, mx * 2 + oc)
     right, left = (tm, xr * 2 + mc), (tm, xl * 2 + mc)
-    after, before = (rem(tm + 1, n_tm), ten), (rem(tm + n_tm - 1, n_tm), ten)
+    sides = (rem(tm + n_tm - 1, n_tm), rem(tm + 1, n_tm))
 
     def offsets(q):
         k, i = div(q, per), rem(q, per)
-        return k + chunks * div(i, NY // 2), 2 * rem(i, NY // 2) + par
+        turn = jnp.int32(ORDER[0])
+        for m in range(1, NZ):
+            turn = turn + (ORDER[m] - ORDER[m - 1]) * div(k + NZ - m, NZ)
+        return rem(2 * i + turn, NZ), 2 * i + par
 
     def dest(q):
         dz, dy = offsets(q)
@@ -154,12 +182,13 @@
 
     for d in range(1, n_t):
         greet(tensor_peer(d))
-    greet(after)
-    greet(before)
+    for side in sides:
+        for d in range(n_t):
+            greet((side, rem(ten + d, n_t)))
 
     @pl.loop(0, chunks * per)
     def _(q):
-        @pl.when(q + par > 0)
+        @pl.when((q != own_q) | (par > 0))
         def _():
             greet(dest(q))
 
@@ -168,26 +197,41 @@
     local_w = [pltpu.make_async_copy(hbm[i], wbuf[i].at[0], s.wl.at[i]) for i in range(3)]
     for copy in local_w:
         copy.start()
+    brought[1].wait()
     row_sums(frames_ref, s.stat_s.at[0], groups)
+    for i in (0, 2, 3, 4, 5, 6):
+        brought[i].wait()
     s.gain_s[...] = jnp.broadcast_to(fgain_ref[...], (8, 128))
-    pl.semaphore_wait(bar, n_t - 1 + 2 + chunks * per - 1 + par)
+    pl.semaphore_wait(bar, n_t - 1 + 2 * n_t + chunks * per - 1 + par)
 
     def stat_copies(phase):
         return [
-            remote(s.stat_s.at[phase], s.stat_r.at[phase, d - 1], s.st_ss.at[phase, d - 1], s.st_rs.at[phase, d - 1], tensor_peer(d))
+            remote(s.stat_s.at[phase], s.stat_r.at[phase, d - 1], s.st_ss.at[phase], s.st_rs.at[phase], tensor_peer(d))
             for d in range(1, n_t)
         ]
 
-    def norm_factors(phase):
-        total = s.stat_s[phase]
-        for d in range(n_t - 1):
-            total = total + s.stat_r[phase, d]
+    def factors(tiles):
+        total = tiles[0]
+        for tile in tiles[1:]:
+            total = total + tile
         mean = total[0:groups] / model
         square = total[groups : 2 * groups] / model
         return mean, lax.rsqrt(square - mean * mean + EPS)
 
+    def norm_factors(phase):
+        return factors([s.stat_s[phase]] + [s.stat_r[phase, d] for d in range(n_t - 1)])
+
     first_stats = stat_copies(0)
-    for copy in first_stats:
+    halos = [
+        remote(s.frames.at[pl.ds(i * (rows - 16), 16)], s.halo_r.at[1 - i], s.edge_ss.at[0], s.edge_rs.at[0], (sides[i], ten))
+        for i in range(2)
+    ]
+    edges = [
+        remote(s.stat_s.at[0], s.edge_r.at[1 - i, d], s.edge_ss.at[1], s.edge_rs.at[1], (sides[i], rem(ten + d, n_t)))
+        for i in range(2)
+        for d in range(n_t)
+    ]
+    for copy in first_stats + halos + edges:
         copy.start()
     gain_copy = remote(s.gain_s, s.gain_r, s.one_ss.at[0], s.one_rs.at[0], partner)
     gain_copy.start()
@@ -228,7 +272,10 @@
         ez, ey = names_k[k] >> 3, names_k[k] & 7
         dz = (ez - mz + NZ) & (NZ - 1)
         dy = (ey - my + NY) & (NY - 1)
-        q = (dz & (chunks - 1)) * per + (dz // chunks) * (NY // 2) + (dy >> 1)
+        turn = jnp.zeros(dz.shape, I32)
+        for m in range(1, NZ):
+            turn = jnp.where(((dz - 2 * (dy >> 1)) & (NZ - 1)) == ORDER[m], m, turn)
+        q = turn * per + (dy >> 1)
         target.append(jnp.where((dy & 1) == par, q * CAP + slot, -1))
     place = lax.broadcasted_iota(I32, (crow, rows), 0)
 
@@ -237,23 +284,13 @@
         here = place + k * crow
         s.pmat[k] = jnp.where((here == target[0]) | (here == target[1]), 1.0, 0.0).astype(BF16)
 
-    for copy in first_stats:
-        copy.wait_recv()
+    wait_all(s.stat_r.at[0], s.st_rs.at[0])
 
     mean, scale = norm_factors(0)
     for g in range(groups):
         x = frames_ref[128 * g : 128 * (g + 1), :].astype(F32)
         n = ((x - spread(mean[g : g + 1])) * spread(scale[g : g + 1]) * cgain_ref[...]).astype(BF16)
         s.nbuf[16 + 128 * g : 16 + 128 * (g + 1), :] = n.astype(F32)
-    s.halo_s[0] = s.nbuf[16:32, :].astype(BF16)
-    s.halo_s[1] = s.nbuf[rows : rows + 16, :].astype(BF16)
-    halos = [
-        remote(s.halo_s.at[0], s.halo_r.at[0], s.halo_ss.at[0], s.halo_rs.at[0], before),
-        remote(s.halo_s.at[1], s.halo_r.at[1], s.halo_ss.at[1], s.halo_rs.at[1], after),
-    ]
-    for copy in halos:
-        copy.start()
-
     block = 64
 
     def conv(r0):
@@ -273,10 +310,14 @@
 
     for r0 in range(block, rows - block, block):
         conv(r0)
-    for copy in halos:
-        copy.wait_recv()
-    s.nbuf[0:16, :] = s.halo_r[1].astype(F32)
-    s.nbuf[rows + 16 : rows + 32, :] = s.halo_r[0].astype(F32)
+    wait_all(s.halo_r, s.edge_rs.at[0])
+    wait_all(s.edge_r, s.edge_rs.at[1])
+    for i, g in enumerate((groups - 1, 0)):
+        mean, scale = factors([s.edge_r[i, d] for d in range(n_t)])
+        span = slice(112, 128) if i == 0 else slice(0, 16)
+        x = s.halo_r[i].astype(F32)
+        n = ((x - spread(mean[g : g + 1])[span]) * spread(scale[g : g + 1])[span] * cgain_ref[...]).astype(BF16)
+        s.nbuf[i * (rows + 16) : i * (rows + 16) + 16, :] = n.astype(F32)
     conv(0)
     conv(rows - block)
 
@@ -295,8 +336,7 @@
 
     gain_copy.wait_recv()
     resid_copy.wait_recv()
-    for copy in second_stats:
-        copy.wait_recv()
+    wait_all(s.stat_r.at[1], s.st_rs.at[1])
     mean, scale = norm_factors(1)
     for g in range(groups):
         m, r = spread(mean[g : g + 1]), spread(scale[g : g + 1])
@@ -305,10 +345,10 @@
         s.ein[oc, lanes, :] = ((s.resid_p[lanes, :] - m) * r * s.gain_r[0:1, :]).astype(BF16)
 
     def send(q):
-        return remote(s.table.at[q], s.gath.at[mx, q], s.a_ss.at[q], s.a_rs.at[q], dest(q))
+        return remote(s.table.at[q], s.gath.at[mx, q], s.a_ss.at[0], s.a_rs.at[div(q, per)], dest(q))
 
     def keep(q):
-        return pltpu.make_async_copy(s.table.at[q], s.gath.at[mx, q], s.a_rs.at[q])
+        return pltpu.make_async_copy(s.table.at[q], s.gath.at[mx, q], s.a_rs.at[div(q, per)])
 
     def pack(value):
         v = jnp.concatenate([value[:, 0:128].reshape(per, CAP, 128), value[:, 128:256].reshape(per, CAP, 128)], axis=1)
@@ -321,20 +361,23 @@
     def per_block(k, remotely, locally):
         @pl.loop(k * per, (k + 1) * per)
         def _(q):
-            @pl.when(q + par > 0)
+            @pl.when((q != own_q) | (par > 0))
             def _():
                 remotely(q)
 
-            @pl.when(q + par == 0)
+            @pl.when((q == own_q) & (par == 0))
             def _():
                 locally(q)
 
-    @pl.loop(0, chunks)
-    def _(k):
+    def dispatch(k):
         both_cols = jnp.concatenate([s.ein[0], s.ein[1]], axis=1)
         picked = jnp.dot(s.pmat[k], both_cols, preferred_element_type=F32)
         s.table[pl.ds(k * per, per)] = pack(picked)
         per_block(k, lambda q: send(q).start(), lambda q: keep(q).start())
+
+    @pl.loop(0, chunks)
+    def _(k):
+        dispatch(k)
 
     @pl.loop(0, chunks)
     def _(k):
@@ -353,7 +396,7 @@
         whole, first, second = pl.ds(k * per, per), pl.ds(k * per, per // 2), pl.ds(k * per + per // 2, per // 2)
 
         def along(x, span, i, dev):
-            return remote(s.gath.at[x, span], s.gath.at[x, span], s.g_ss.at[k, i], s.g_rs.at[k, i], dev)
+            return remote(s.gath.at[x, span], s.gath.at[x, span], s.g_ss.at[0], s.g_rs.at[k, i // 2], dev)
 
         return (
             along(mx, whole, 0, right),
@@ -363,13 +406,13 @@
         )
 
     def sum_copy(k, way, i):
-        return remote(s.rs_s.at[k, way, i], s.rs_r.at[k, way, i], s.r_ss.at[k, way, i], s.r_rs.at[k, way, i], (right, left)[way])
+        return remote(s.rs_s.at[k, i, way], s.rs_r.at[k, i, way], s.r_ss.at[0], s.r_rs.at[k, min(i, 1)], (right, left)[way])
 
     def send_back(q):
-        return remote(s.back.at[q], s.ret.at[q], s.b_ss.at[q], s.b_rs.at[q], source(q))
+        return remote(s.back.at[q], s.ret.at[q], s.b_ss.at[0], s.b_rs.at[div(q, per)], source(q))
 
     def keep_back(q):
-        return pltpu.make_async_copy(s.back.at[q], s.ret.at[q], s.b_rs.at[q])
+        return pltpu.make_async_copy(s.back.at[q], s.ret.at[q], s.b_rs.at[div(q, per)])
 
     for copy in local_w:
         copy.wait()
@@ -377,22 +420,19 @@
         copy.wait_recv()
 
     def arrive(k):
-        per_block(k, lambda q: send(q).wait_recv(), lambda q: keep(q).wait())
+        wait_all(s.gath.at[mx, pl.ds(k * per, per)], s.a_rs.at[k])
         to_right, to_left, _, _ = gather_copies(k)
         to_right.start()
         to_left.start()
 
     def forward(k):
-        to_right, to_left, on_right, on_left = gather_copies(k)
-        to_right.wait_recv()
+        _, _, on_right, on_left = gather_copies(k)
+        wait_all(s.gath.at[pl.ds(0, 2), pl.ds(k * per, per)], s.g_rs.at[k, 0])
         on_right.start()
-        to_left.wait_recv()
         on_left.start()
 
     def experts_of(k):
-        _, _, on_right, on_left = gather_copies(k)
-        on_right.wait_recv()
-        on_left.wait_recv()
+        wait_all(s.gath.at[0, pl.ds(k * per, per)], s.g_rs.at[k, 1])
         for x in range(NX):
             low, high = unpack(s.gath[x, pl.ds(k * per, per)])
             s.abuf[:, 256 * x : 256 * x + 128] = low
@@ -409,32 +449,29 @@
             s.ybuf[k, n] = y + jnp.dot(s.hbuf[:, hid:], s.wd[1, :, cols], preferred_element_type=F32)
         s.rs_s[k, 0, 0] = s.ybuf[k, xo, 0:hrow, :].astype(BF16)
         sum_copy(k, 0, 0).start()
-        s.rs_s[k, 1, 0] = s.ybuf[k, xo, hrow:crow, :].astype(BF16)
+        s.rs_s[k, 0, 1] = s.ybuf[k, xo, hrow:crow, :].astype(BF16)
         sum_copy(k, 1, 0).start()
-        s.rs_s[k, 0, 1] = s.ybuf[k, xr, hrow:crow, :].astype(BF16)
+        s.rs_s[k, 1, 0] = s.ybuf[k, xr, hrow:crow, :].astype(BF16)
         sum_copy(k, 0, 1).start()
         s.rs_s[k, 1, 1] = s.ybuf[k, xl, 0:hrow, :].astype(BF16)
         sum_copy(k, 1, 1).start()
 
     def pass_on(k):
-        sum_copy(k, 0, 0).wait_recv()
-        s.rs_s[k, 0, 2] = (s.ybuf[k, xr, 0:hrow, :] + s.rs_r[k, 0, 0].astype(F32)).astype(BF16)
+        wait_all(s.rs_r.at[k, 0], s.r_rs.at[k, 0])
+        s.rs_s[k, 2, 0] = (s.ybuf[k, xr, 0:hrow, :] + s.rs_r[k, 0, 0].astype(F32)).astype(BF16)
         sum_copy(k, 0, 2).start()
-        sum_copy(k, 1, 0).wait_recv()
-        s.rs_s[k, 1, 2] = (s.ybuf[k, xl, hrow:crow, :] + s.rs_r[k, 1, 0].astype(F32)).astype(BF16)
+        s.rs_s[k, 2, 1] = (s.ybuf[k, xl, hrow:crow, :] + s.rs_r[k, 0, 1].astype(F32)).astype(BF16)
         sum_copy(k, 1, 2).start()
 
     def finish(k):
-        for way in range(2):
-            sum_copy(k, way, 1).wait_recv()
-            sum_copy(k, way, 2).wait_recv()
-        top = s.ybuf[k, mx, 0:hrow, :] + s.rs_r[k, 0, 2].astype(F32) + s.rs_r[k, 1, 1].astype(F32)
-        low = s.ybuf[k, mx, hrow:crow, :] + s.rs_r[k, 1, 2].astype(F32) + s.rs_r[k, 0, 1].astype(F32)
+        wait_all(s.rs_r.at[k, pl.ds(1, 2)], s.r_rs.at[k, 1])
+        top = s.ybuf[k, mx, 0:hrow, :] + s.rs_r[k, 2, 0].astype(F32) + s.rs_r[k, 1, 1].astype(F32)
+        low = s.ybuf[k, mx, hrow:crow, :] + s.rs_r[k, 2, 1].astype(F32) + s.rs_r[k, 1, 0].astype(F32)
         s.back[pl.ds(k * per, per)] = pack(jnp.concatenate([top, low], axis=0))
         per_block(k, lambda q: send_back(q).start(), lambda q: keep_back(q).start())
 
     def combine(k):
-        per_block(k, lambda q: send_back(q).wait_recv(), lambda q: keep_back(q).wait())
+        wait_all(s.ret.at[pl.ds(k * per, per)], s.b_rs.at[k])
         low, high = unpack(s.ret[pl.ds(k * per, per)])
         both_cols = jnp.concatenate([low, high], axis=1)
         mixed = jnp.dot(s.wmat[k, 0], both_cols, preferred_element_type=F32)
@@ -447,14 +484,14 @@
         def _():
             stage(step - lag)
 
-    @pl.loop(0, chunks + 5)
+    @pl.loop(0, chunks + LAGS[4])
     def _(step):
         at(step, 0, arrive)
-        at(step, 1, forward)
-        at(step, 3, pass_on)
-        at(step, 4, finish)
-        at(step, 2, experts_of)
-        at(step, 5, combine)
+        at(step, LAGS[0], forward)
+        at(step, LAGS[2], pass_on)
+        at(step, LAGS[3], finish)
+        at(step, LAGS[1], experts_of)
+        at(step, LAGS[4], combine)
 
     mix_copy = remote(s.macc.at[oc], s.mix_r, s.one_ss.at[2], s.one_rs.at[2], partner)
     mix_copy.start()
@@ -462,32 +499,33 @@
     mix_copy.wait_recv()
     out_ref[...] = (own + s.mix_r[...]).astype(BF16)
 
-    for copy in first_stats + second_stats + [gain_copy, resid_copy, mix_copy] + remote_w + halos:
+    for copy in [gain_copy, resid_copy, mix_copy] + remote_w:
         copy.wait_send()
-
-    def left_q(q):
-        send(q).wait_send()
-        send_back(q).wait_send()
-
-    @pl.loop(0, chunks)
-    def _(k):
-        per_block(k, left_q, lambda q: None)
-        for copy in gather_copies(k):
-            copy.wait_send()
-        for way in range(2):
-            for i in range(3):
-                sum_copy(k, way, i).wait_send()
+    for phase in range(2):
+        wait_all(s.stat_r.at[phase], s.st_ss.at[phase])
+    wait_all(s.halo_r, s.edge_ss.at[0])
+    wait_all(s.edge_r, s.edge_ss.at[1])
+    wait_all(s.gath.at[pl.ds(0, 3)], s.g_ss.at[0])
+    wait_all(s.rs_s, s.r_ss.at[0])
+    others = chunks * per - 1
+    wait_all(s.table.at[pl.ds(0, others)], s.a_ss.at[0])
+    wait_all(s.back.at[pl.ds(0, others)], s.b_ss.at[0])
+
+    @pl.when(par > 0)
+    def _():
+        wait_all(s.table.at[0], s.a_ss.at[0])
+        wait_all(s.back.at[0], s.b_ss.at[0])
 
 
 def shards(frames, conv_kernel, conv_gain, ffn_gain, lengths, routes, route_weights, w_gate, w_up, w_down):
     rows, width = frames.shape
     _, depth, hid = w_gate.shape
-    scratch = names(rows, width, hid, depth, conv_kernel.shape[0])
+    scratch = names(rows, width, hid, depth, conv_kernel.shape[0], lengths.shape[0])
     vmem = pl.BlockSpec(memory_space=pltpu.VMEM)
     return pl.pallas_call(
         functools.partial(kernel, tuple(scratch)),
         out_shape=jax.ShapeDtypeStruct((rows, width), BF16),
-        in_specs=[pl.BlockSpec(memory_space=pltpu.SMEM)] + [vmem] * 6 + [pl.BlockSpec(memory_space=pl.ANY)] * 3,
+        in_specs=[pl.BlockSpec(memory_space=pl.ANY)] * 10,
         out_specs=vmem,
         scratch_shapes=list(scratch.values()),
         compiler_params=pltpu.CompilerParams(collective_id=0, has_side_effects=True, vmem_limit_bytes=56 * 1024 * 1024),

time: 85.7 us -> 76.1 us (0.89)
  Pallas kernels: 83.9 us -> 74.4 us
    pallas_call x1, Pallas kernels: 83.9 us -> 74.4 us  [shards(): pl.pallas_call(functools.partial(kernel, tuple(scratch)), out_shape=jax.S...]
where the time goes in v2:
time: 76.1 us; the launch traced here: 76 us
  Pallas kernels  74.4 us (98%)
  local copies, waits for them, and re-layouts  1.57 us (2%)
    pallas_call x1, Pallas kernels, shards(): pl.pallas_call(functools.partial(kernel, tuple(scratch)), out_shape=jax.S...  74.4 us
    unnamed x1, local copies, waits for them, and re-layouts  1.57 us

profile of v2, /device:TPU:1, one launch (start us, length us, event | category | flops | bytes accessed | tf_op | source)
XLA Modules:
  0.0 76.0 jit_solution(14415231612446356436)
XLA Ops:
  0.0 74.4 %shard_map.100 = bf16[512,128]{1,0:T(8,128)(2,1)} custom-call(s32[8]{0:T(128)} %refs_0_.1, bf16[512,128]{1,0:T(8,128)(2,1)} %refs_1_.1, bf16[31,128]{1,0:T(8,128)(2,1)} %refs_2_.1, f32[1,128]{1,0:T(1,128)} %bitcast.12, f32[1,128]{1,0:T(1,128)} %bitcast.13, s32[2,512]{1,0:T(2,128)} %bitcast.10, f32[2,512]{1,0:T(2,128)} %bitcast.11, ...), custom_call_target="tpu_custom_call" | custom-call | tf_op jit(solution)/shard_map/pallas_call | solution.py:525
  74.4 1.6 %copy.12 = bf16[512,128]{1,0:T(8,128)(2,1)} copy(bf16[512,128]{1,0:T(8,128)(2,1)} %shard_map.100) | data formatting | bytes 262144

commit v3 on v2

--- a/solution.py
+++ b/solution.py
@@ -14,8 +14,10 @@
 NX = 4
 NZ = 8
 NY = 8
-ORDER = (4, 3, 2, 0, 1, 7, 6, 5)
-LAGS = (2, 6, 9, 12, 17)
+ORDER = (6, 5, 2, 1, 0, 7, 3, 4)
+EARLY = 2
+SEND_EARLY = 3
+LAGS = (2, 5, 8, 11, 16)
 F32 = jnp.float32
 BF16 = jnp.bfloat16
 I32 = jnp.int32
@@ -85,7 +87,8 @@
         "dcol": vm((2, rows, 128), I32),
         "wcol": vm((2, rows, 128), F32),
         "wmat": vm((chunks, 2, rows, crow), BF16),
-        "table": vm((q, 2 * CAP, 128), BF16),
+        "table": vm((q - EARLY * per, 2 * CAP, 128), BF16),
+        "pre": vm((NX, EARLY * per, 2 * CAP, 128), BF16),
         "gath": vm((NX, q, 2 * CAP, 128), BF16),
         "wg": vm((2, model, hid), BF16),
         "wu": vm((2, model, hid), BF16),
@@ -108,10 +111,12 @@
         "wl": sem((3,)),
         "w_ss": sem((3,)),
         "w_rs": sem((3,)),
-        "a_ss": sem((1,)),
+        "p_ss": sem((1,)),
+        "p_rs": sem((2,)),
+        "a_ss": sem((2,)),
         "a_rs": sem((chunks,)),
         "g_ss": sem((1,)),
-        "g_rs": sem((chunks, 2)),
+        "g_rs": sem((chunks - EARLY, 2)),
         "r_ss": sem((1,)),
         "r_rs": sem((chunks, 2)),
         "b_ss": sem((1,)),
@@ -150,27 +155,42 @@
     mx, mc = div(ten, 2), rem(ten, 2)
     oc = 1 - mc
     par = rem(my + mc, 2)
-    own_q = ORDER.index(0) * per
+    own_k = ORDER.index(0)
+    late = chunks - EARLY
     xr, xl, xo = rem(mx + 1, NX), rem(mx + NX - 1, NX), rem(mx + 2, NX)
     peer_t = mx * 2 + rem(my, 2)
     partner = (tm, mx * 2 + oc)
     right, left = (tm, xr * 2 + mc), (tm, xl * 2 + mc)
     sides = (rem(tm + n_tm - 1, n_tm), rem(tm + 1, n_tm))
 
-    def offsets(q):
-        k, i = div(q, per), rem(q, per)
+    def turn_of(k):
         turn = jnp.int32(ORDER[0])
         for m in range(1, NZ):
             turn = turn + (ORDER[m] - ORDER[m - 1]) * div(k + NZ - m, NZ)
-        return rem(2 * i + turn, NZ), 2 * i + par
-
-    def dest(q):
-        dz, dy = offsets(q)
-        return (rem(mz + dz, NZ) * NY + rem(my + dy, NY), peer_t)
-
-    def source(q):
-        dz, dy = offsets(q)
-        return (rem(mz + NZ - dz, NZ) * NY + rem(my + NY - dy, NY), peer_t)
+        return turn
+
+    def dest(turn, i):
+        return (rem(mz + 2 * i + turn, NZ) * NY + rem(my + 2 * i + par, NY), peer_t)
+
+    def source(turn, i):
+        return (rem(mz + 2 * NZ - 2 * i - turn, NZ) * NY + rem(my + 2 * NY - 2 * i - par, NY), peer_t)
+
+    def per_block(k, remotely, locally=None):
+        turn = turn_of(k)
+        for i in range(per):
+            if i > 0:
+                remotely(k, turn, i)
+                continue
+
+            @pl.when((k != own_k) | (par > 0))
+            def _():
+                remotely(k, turn, 0)
+
+            if locally is not None:
+
+                @pl.when((k == own_k) & (par == 0))
+                def _():
+                    locally(k)
 
     def tensor_peer(d):
         return (tm, rem(ten + d, n_t))
@@ -186,11 +206,9 @@
         for d in range(n_t):
             greet((side, rem(ten + d, n_t)))
 
-    @pl.loop(0, chunks * per)
-    def _(q):
-        @pl.when((q != own_q) | (par > 0))
-        def _():
-            greet(dest(q))
+    @pl.loop(0, chunks)
+    def _(k):
+        per_block(k, lambda k, turn, i: greet(dest(turn, i)))
 
     hbm = (wg_hbm, wu_hbm, wd_hbm)
     wbuf = (s.wg, s.wu, s.wd)
@@ -344,11 +362,12 @@
         s.ein[mc, lanes, :] = ((s.resid[lanes, :] - m) * r * fgain_ref[...]).astype(BF16)
         s.ein[oc, lanes, :] = ((s.resid_p[lanes, :] - m) * r * s.gain_r[0:1, :]).astype(BF16)
 
-    def send(q):
-        return remote(s.table.at[q], s.gath.at[mx, q], s.a_ss.at[0], s.a_rs.at[div(q, per)], dest(q))
-
-    def keep(q):
-        return pltpu.make_async_copy(s.table.at[q], s.gath.at[mx, q], s.a_rs.at[div(q, per)])
+    def send(k, turn, i):
+        q = k * per + i
+        remote(s.table.at[q], s.gath.at[mx, q], s.a_ss.at[0], s.a_rs.at[k], dest(turn, i)).start()
+
+    def keep(k):
+        pltpu.make_async_copy(s.table.at[k * per], s.gath.at[mx, k * per], s.a_rs.at[k]).start()
 
     def pack(value):
         v = jnp.concatenate([value[:, 0:128].reshape(per, CAP, 128), value[:, 128:256].reshape(per, CAP, 128)], axis=1)
@@ -358,24 +377,30 @@
         v = value.astype(F32)
         return v[:, :CAP, :].reshape(crow, 128).astype(BF16), v[:, CAP:, :].reshape(crow, 128).astype(BF16)
 
-    def per_block(k, remotely, locally):
-        @pl.loop(k * per, (k + 1) * per)
-        def _(q):
-            @pl.when((q != own_q) | (par > 0))
-            def _():
-                remotely(q)
-
-            @pl.when((q == own_q) & (par == 0))
-            def _():
-                locally(q)
+    def picked(k):
+        both_cols = jnp.concatenate([s.ein[0], s.ein[1]], axis=1)
+        return pack(jnp.dot(s.pmat[k], both_cols, preferred_element_type=F32))
+
+    def early_copy(x, span, i, dev):
+        return remote(s.pre.at[x, span], s.pre.at[x, span], s.p_ss.at[0], s.p_rs.at[i], dev)
+
+    def send_early(k, turn, i):
+        q = k * per + i
+        remote(s.pre.at[:, q - late * per], s.gath.at[:, q], s.a_ss.at[1], s.a_rs.at[k], dest(turn, i)).start()
+
+    @pl.loop(late, chunks)
+    def _(k):
+        s.pre[mx, pl.ds((k - late) * per, per)] = picked(k)
+
+    n_early = EARLY * per
+    early_copy(mx, pl.ds(0, n_early), 0, right).start()
+    early_copy(mx, pl.ds(0, n_early), 0, left).start()
 
     def dispatch(k):
-        both_cols = jnp.concatenate([s.ein[0], s.ein[1]], axis=1)
-        picked = jnp.dot(s.pmat[k], both_cols, preferred_element_type=F32)
-        s.table[pl.ds(k * per, per)] = pack(picked)
-        per_block(k, lambda q: send(q).start(), lambda q: keep(q).start())
-
-    @pl.loop(0, chunks)
+        s.table[pl.ds(k * per, per)] = picked(k)
+        per_block(k, send, keep)
+
+    @pl.loop(0, late)
     def _(k):
         dispatch(k)
 
@@ -408,16 +433,24 @@
     def sum_copy(k, way, i):
         return remote(s.rs_s.at[k, i, way], s.rs_r.at[k, i, way], s.r_ss.at[0], s.r_rs.at[k, min(i, 1)], (right, left)[way])
 
-    def send_back(q):
-        return remote(s.back.at[q], s.ret.at[q], s.b_ss.at[0], s.b_rs.at[div(q, per)], source(q))
-
-    def keep_back(q):
-        return pltpu.make_async_copy(s.back.at[q], s.ret.at[q], s.b_rs.at[div(q, per)])
+    def send_back(k, turn, i):
+        q = k * per + i
+        remote(s.back.at[q], s.ret.at[q], s.b_ss.at[0], s.b_rs.at[k], source(turn, i)).start()
+
+    def keep_back(k):
+        pltpu.make_async_copy(s.back.at[k * per], s.ret.at[k * per], s.b_rs.at[k]).start()
 
     for copy in local_w:
         copy.wait()
     for copy in remote_w:
         copy.wait_recv()
+
+    def leave_early():
+        wait_all(s.pre.at[0], s.p_rs.at[1])
+
+        @pl.loop(late, chunks)
+        def _(k):
+            per_block(k, send_early)
 
     def arrive(k):
         wait_all(s.gath.at[mx, pl.ds(k * per, per)], s.a_rs.at[k])
@@ -432,7 +465,14 @@
         on_left.start()
 
     def experts_of(k):
-        wait_all(s.gath.at[0, pl.ds(k * per, per)], s.g_rs.at[k, 1])
+        @pl.when(k < late)
+        def _():
+            wait_all(s.gath.at[0, pl.ds(k * per, per)], s.g_rs.at[k, 1])
+
+        @pl.when(k >= late)
+        def _():
+            wait_all(s.gath.at[:, pl.ds(k * per, per)], s.a_rs.at[k])
+
         for x in range(NX):
             low, high = unpack(s.gath[x, pl.ds(k * per, per)])
             s.abuf[:, 256 * x : 256 * x + 128] = low
@@ -468,7 +508,7 @@
         top = s.ybuf[k, mx, 0:hrow, :] + s.rs_r[k, 2, 0].astype(F32) + s.rs_r[k, 1, 1].astype(F32)
         low = s.ybuf[k, mx, hrow:crow, :] + s.rs_r[k, 2, 1].astype(F32) + s.rs_r[k, 1, 0].astype(F32)
         s.back[pl.ds(k * per, per)] = pack(jnp.concatenate([top, low], axis=0))
-        per_block(k, lambda q: send_back(q).start(), lambda q: keep_back(q).start())
+        per_block(k, send_back, keep_back)
 
     def combine(k):
         wait_all(s.ret.at[pl.ds(k * per, per)], s.b_rs.at[k])
@@ -479,15 +519,20 @@
         s.macc[0] += mixed[:, 0:128]
         s.macc[1] += mixed[:, 128:256]
 
-    def at(step, lag, stage):
-        @pl.when((step >= lag) & (step < lag + chunks))
+    def at(step, lag, stage, count=chunks):
+        @pl.when((step >= lag) & (step < lag + count))
         def _():
             stage(step - lag)
 
+    wait_all(s.pre.at[pl.ds(0, 2)], s.p_rs.at[0])
+    early_copy(xl, pl.ds(0, n_early // 2), 1, right).start()
+    early_copy(xr, pl.ds(n_early // 2, n_early // 2), 1, left).start()
+
     @pl.loop(0, chunks + LAGS[4])
     def _(step):
-        at(step, 0, arrive)
-        at(step, LAGS[0], forward)
+        pl.when(step == SEND_EARLY)(leave_early)
+        at(step, 0, arrive, late)
+        at(step, LAGS[0], forward, late)
         at(step, LAGS[2], pass_on)
         at(step, LAGS[3], finish)
         at(step, LAGS[1], experts_of)
@@ -505,11 +550,12 @@
         wait_all(s.stat_r.at[phase], s.st_ss.at[phase])
     wait_all(s.halo_r, s.edge_ss.at[0])
     wait_all(s.edge_r, s.edge_ss.at[1])
-    wait_all(s.gath.at[pl.ds(0, 3)], s.g_ss.at[0])
+    wait_all(s.gath.at[pl.ds(0, 3), pl.ds(0, late * per)], s.g_ss.at[0])
+    wait_all(s.pre.at[pl.ds(0, 3)], s.p_ss.at[0])
+    wait_all(s.pre, s.a_ss.at[1])
     wait_all(s.rs_s, s.r_ss.at[0])
-    others = chunks * per - 1
-    wait_all(s.table.at[pl.ds(0, others)], s.a_ss.at[0])
-    wait_all(s.back.at[pl.ds(0, others)], s.b_ss.at[0])
+    wait_all(s.table.at[pl.ds(0, late * per - 1)], s.a_ss.at[0])
+    wait_all(s.back.at[pl.ds(0, chunks * per - 1)], s.b_ss.at[0])
 
     @pl.when(par > 0)
     def _():

time: 76.1 us -> 73.9 us (0.971)
  Pallas kernels: 74.4 us -> 72.2 us
    pallas_call x1, Pallas kernels: 74.4 us -> 72.2 us  [shards(): pl.pallas_call(functools.partial(kernel, tuple(scratch)), out_shape=jax.S...]
where the time goes in v3:
time: 73.9 us; the launch traced here: 73.7 us
  Pallas kernels  72.2 us (98%)
  local copies, waits for them, and re-layouts  1.57 us (2%)
    pallas_call x1, Pallas kernels, shards(): pl.pallas_call(functools.partial(kernel, tuple(scratch)), out_shape=jax.S...  72.2 us
    unnamed x1, local copies, waits for them, and re-layouts  1.57 us

profile of v3, /device:TPU:1, one launch (start us, length us, event | category | flops | bytes accessed | tf_op | source)
XLA Modules:
  0.0 73.7 jit_solution(10531779524982416448)
XLA Ops:
  0.0 72.2 %shard_map.100 = bf16[512,128]{1,0:T(8,128)(2,1)} custom-call(s32[8]{0:T(128)} %refs_0_.1, bf16[512,128]{1,0:T(8,128)(2,1)} %refs_1_.1, bf16[31,128]{1,0:T(8,128)(2,1)} %refs_2_.1, f32[1,128]{1,0:T(1,128)} %bitcast.12, f32[1,128]{1,0:T(1,128)} %bitcast.13, s32[2,512]{1,0:T(2,128)} %bitcast.10, f32[2,512]{1,0:T(2,128)} %bitcast.11, ...), custom_call_target="tpu_custom_call" | custom-call | tf_op jit(solution)/shard_map/pallas_call | solution.py:571
  72.2 1.6 %copy.12 = bf16[512,128]{1,0:T(8,128)(2,1)} copy(bf16[512,128]{1,0:T(8,128)(2,1)} %shard_map.100) | data formatting | bytes 262144

commit v4 on v3

--- a/solution.py
+++ b/solution.py
@@ -14,10 +14,10 @@
 NX = 4
 NZ = 8
 NY = 8
-ORDER = (6, 5, 2, 1, 0, 7, 3, 4)
+ORDER = (0, 7, 1, 3, 5, 2, 6, 4)
 EARLY = 2
-SEND_EARLY = 3
-LAGS = (2, 5, 8, 11, 16)
+SEND_EARLY = 2
+LAGS = (3, 6, 9, 12, 21)
 F32 = jnp.float32
 BF16 = jnp.bfloat16
 I32 = jnp.int32

time: 73.9 us -> 72.6 us (0.982)
  Pallas kernels: 72.2 us -> 70.9 us
    pallas_call x1, Pallas kernels: 72.2 us -> 70.9 us  [shards(): pl.pallas_call(functools.partial(kernel, tuple(scratch)), out_shape=jax.S...]
where the time goes in v4:
time: 72.6 us; the launch traced here: 72.5 us
  Pallas kernels  70.9 us (98%)
  local copies, waits for them, and re-layouts  1.57 us (2%)
    pallas_call x1, Pallas kernels, shards(): pl.pallas_call(functools.partial(kernel, tuple(scratch)), out_shape=jax.S...  70.9 us
    unnamed x1, local copies, waits for them, and re-layouts  1.57 us

profile of v4, /device:TPU:1, one launch (start us, length us, event | category | flops | bytes accessed | tf_op | source)
XLA Modules:
  0.0 72.5 jit_solution(13912626465843734992)
XLA Ops:
  0.0 70.9 %shard_map.100 = bf16[512,128]{1,0:T(8,128)(2,1)} custom-call(s32[8]{0:T(128)} %refs_0_.1, bf16[512,128]{1,0:T(8,128)(2,1)} %refs_1_.1, bf16[31,128]{1,0:T(8,128)(2,1)} %refs_2_.1, f32[1,128]{1,0:T(1,128)} %bitcast.12, f32[1,128]{1,0:T(1,128)} %bitcast.13, s32[2,512]{1,0:T(2,128)} %bitcast.10, f32[2,512]{1,0:T(2,128)} %bitcast.11, ...), custom_call_target="tpu_custom_call" | custom-call | tf_op jit(solution)/shard_map/pallas_call | solution.py:571
  70.9 1.6 %copy.12 = bf16[512,128]{1,0:T(8,128)(2,1)} copy(bf16[512,128]{1,0:T(8,128)(2,1)} %shard_map.100) | data formatting | bytes 262144

commit v5 on v4

--- a/solution.py
+++ b/solution.py
@@ -101,16 +101,15 @@
         "back": vm((q, 2 * CAP, 128), BF16),
         "ret": vm((q, 2 * CAP, 128), BF16),
         "macc": vm((2, rows, 128), F32),
-        "mix_r": vm((rows, 128), F32),
+        "mix_s": vm((rows, 128), BF16),
+        "mix_r": vm((rows, 128), BF16),
         "st_ss": sem((2,)),
         "st_rs": sem((2,)),
         "one_ss": sem((3,)),
         "one_rs": sem((3,)),
         "edge_ss": sem((2,)),
         "edge_rs": sem((2,)),
-        "wl": sem((3,)),
-        "w_ss": sem((3,)),
-        "w_rs": sem((3,)),
+        "w_sem": sem((3,)),
         "p_ss": sem((1,)),
         "p_rs": sem((2,)),
         "a_ss": sem((2,)),
@@ -212,7 +211,7 @@
 
     hbm = (wg_hbm, wu_hbm, wd_hbm)
     wbuf = (s.wg, s.wu, s.wd)
-    local_w = [pltpu.make_async_copy(hbm[i], wbuf[i].at[0], s.wl.at[i]) for i in range(3)]
+    local_w = [pltpu.make_async_copy(hbm[i], wbuf[i].at[0], s.w_sem.at[0]) for i in range(3)]
     for copy in local_w:
         copy.start()
     brought[1].wait()
@@ -253,7 +252,7 @@
         copy.start()
     gain_copy = remote(s.gain_s, s.gain_r, s.one_ss.at[0], s.one_rs.at[0], partner)
     gain_copy.start()
-    remote_w = [remote(hbm[i], wbuf[i].at[1], s.w_ss.at[i], s.w_rs.at[i], partner) for i in range(3)]
+    remote_w = [remote(hbm[i], wbuf[i].at[1], s.w_sem.at[1], s.w_sem.at[2], partner) for i in range(3)]
     for copy in remote_w:
         copy.start()
 
@@ -440,10 +439,8 @@
     def keep_back(k):
         pltpu.make_async_copy(s.back.at[k * per], s.ret.at[k * per], s.b_rs.at[k]).start()
 
-    for copy in local_w:
-        copy.wait()
-    for copy in remote_w:
-        copy.wait_recv()
+    wait_all(s.ybuf, s.w_sem.at[0])
+    wait_all(s.ybuf, s.w_sem.at[2])
 
     def leave_early():
         wait_all(s.pre.at[0], s.p_rs.at[1])
@@ -538,14 +535,16 @@
         at(step, LAGS[1], experts_of)
         at(step, LAGS[4], combine)
 
-    mix_copy = remote(s.macc.at[oc], s.mix_r, s.one_ss.at[2], s.one_rs.at[2], partner)
+    s.mix_s[...] = s.macc[oc].astype(BF16)
+    mix_copy = remote(s.mix_s, s.mix_r, s.one_ss.at[2], s.one_rs.at[2], partner)
     mix_copy.start()
     own = s.resid[...] + s.macc[mc]
     mix_copy.wait_recv()
-    out_ref[...] = (own + s.mix_r[...]).astype(BF16)
-
-    for copy in [gain_copy, resid_copy, mix_copy] + remote_w:
+    out_ref[...] = (own + s.mix_r[...].astype(F32)).astype(BF16)
+
+    for copy in [gain_copy, resid_copy, mix_copy]:
         copy.wait_send()
+    wait_all(s.ybuf, s.w_sem.at[1])
     for phase in range(2):
         wait_all(s.stat_r.at[phase], s.st_ss.at[phase])
     wait_all(s.halo_r, s.edge_ss.at[0])

time: 72.6 us -> 72.4 us (level)
  no operation moved by 1% of the time
where the time goes in v5:
time: 72.4 us; the launch traced here: 72.2 us
  Pallas kernels  70.7 us (98%)
  local copies, waits for them, and re-layouts  1.57 us (2%)
    pallas_call x1, Pallas kernels, shards(): pl.pallas_call(functools.partial(kernel, tuple(scratch)), out_shape=jax.S...  70.7 us
    unnamed x1, local copies, waits for them, and re-layouts  1.57 us

profile of v5, /device:TPU:1, one launch (start us, length us, event | category | flops | bytes accessed | tf_op | source)
XLA Modules:
  0.0 72.2 jit_solution(12921949174792978779)
XLA Ops:
  0.0 70.7 %shard_map.100 = bf16[512,128]{1,0:T(8,128)(2,1)} custom-call(s32[8]{0:T(128)} %refs_0_.1, bf16[512,128]{1,0:T(8,128)(2,1)} %refs_1_.1, bf16[31,128]{1,0:T(8,128)(2,1)} %refs_2_.1, f32[1,128]{1,0:T(1,128)} %bitcast.12, f32[1,128]{1,0:T(1,128)} %bitcast.13, s32[2,512]{1,0:T(2,128)} %bitcast.10, f32[2,512]{1,0:T(2,128)} %bitcast.11, ...), custom_call_target="tpu_custom_call" | custom-call | tf_op jit(solution)/shard_map/pallas_call | solution.py:570
  70.7 1.6 %copy.12 = bf16[512,128]{1,0:T(8,128)(2,1)} copy(bf16[512,128]{1,0:T(8,128)(2,1)} %shard_map.100) | data formatting | bytes 262144
